TPU v7x, 512 devices: a whole 4x4x16 slice. The times are simulated.
512 devices in a mesh: ctx: 32 (over y_lo, z), head: 8 (over x, core), grp: 2 (over y_hi).
Axes of the slice: x: 4, y: 4 (y_hi: 2, y_lo: 2; y = y_hi * 2 + y_lo), z: 16, core: 2. Of those that a mesh axis runs over, the one named last changes fastest.
Arguments:
- tokens: bfloat16 [2, 8192, 3072], P('grp', 'ctx', 'head'), may hold values from -6 to 6
- modulation: bfloat16 [2, 3, 3072], P('grp'), may hold values from -3 to 3
- w_qkv: bfloat16 [3072, 3, 2048], P(('ctx', 'grp'), None, 'head'), may hold values from -0.09021098 to 0.09021098
- query_gain: float32 [128], replicated, may hold values from 1 to 6
- key_gain: float32 [128], replicated, may hold values from 1 to 6
- w_out: bfloat16 [2048, 3072], P('head'), may hold values from -0.125 to 0.125
Outputs:
- branch: bfloat16 [2, 8192, 3072], P('grp', 'ctx', 'head')
All inputs are finite; a program needn't handle non-finite values.
Results may differ from a plain program's by a relative error of at most 0.02.
The roundings to bfloat16 on the way count: a program that leaves them out, or rounds other values in their place, can miss the bound.
Values may be sent and summed in bfloat16 or wider, within the bound.
A program may use at most 64 MiB of HBM per device.

v0:
```python
import jax
import jax.numpy as jnp
from jax import lax
from jax.sharding import PartitionSpec as P

HDIM = 128


def norm_heads(values, gain):
    mean_square = jnp.mean(values * values, axis=-1, keepdims=True)
    return (values * lax.rsqrt(mean_square + 1e-06) * gain).astype(jnp.bfloat16)


def attend_all(queries):
    scaling = HDIM ** (-0.5)

    def block_update(state, block_keys, block_values):
        highest, totals, summed = state
        scores = (
            jnp.einsum("qhd,khd->hqk", queries, block_keys, preferred_element_type=jnp.float32)
            * scaling
        )
        newest = jnp.maximum(highest, jnp.max(scores, axis=-1))
        factor = jnp.exp(highest - newest)
        weights = jnp.exp(scores - newest[..., None])
        totals = totals * factor + jnp.sum(weights, axis=-1)
        update = jnp.einsum(
            "hqk,khd->hqd",
            weights.astype(jnp.bfloat16),
            block_values,
            preferred_element_type=jnp.float32,
        )
        return (newest, totals, summed * factor[..., None] + update)

    def fold_keys(state, pieces, begin):
        piece_keys, piece_values = pieces
        count = piece_keys.shape[0]
        blocked_keys = piece_keys.reshape(
            count // 512, 512, piece_keys.shape[1], piece_keys.shape[2]
        )
        blocked_values = piece_values.reshape(
            count // 512, 512, piece_values.shape[1], piece_values.shape[2]
        )

        def step_block(inner, pair):
            return (block_update(inner, pair[0], pair[1]), None)

        state, unused = lax.scan(step_block, state, (blocked_keys, blocked_values))
        return state

    return fold_keys


def body(tokens, modulation, w_qkv, query_gain, key_gain, w_out):
    local_tokens = tokens.shape[1]
    local_heads = w_qkv.shape[2] // HDIM
    whole = lax.all_gather(tokens[0], "head", axis=1, tiled=True)
    floats = whole.astype(jnp.float32)
    center = jnp.mean(floats, axis=-1, keepdims=True)
    spread = jnp.mean((floats - center) ** 2, axis=-1, keepdims=True)
    normed = (floats - center) * lax.rsqrt(spread + 1e-06)
    mods = modulation[0].astype(jnp.float32)
    modulated = (normed * (1.0 + mods[1]) + mods[0]).astype(jnp.bfloat16)
    weight_rows = w_qkv.reshape(w_qkv.shape[0], 3 * w_qkv.shape[2])
    columns = modulated
    qkv = jnp.dot(
        columns,
        lax.all_gather(weight_rows, ("ctx", "grp"), axis=0, tiled=True),
        preferred_element_type=jnp.float32,
    )
    qkv = qkv.reshape(local_tokens, 3, local_heads, HDIM)
    queries = norm_heads(qkv[:, 0], query_gain)
    keys = norm_heads(qkv[:, 1], key_gain)
    values = qkv[:, 2].astype(jnp.bfloat16)
    start_state = (
        jnp.full((local_heads, local_tokens), -1e30, jnp.float32),
        jnp.zeros((local_heads, local_tokens), jnp.float32),
        jnp.zeros((local_heads, local_tokens, HDIM), jnp.float32),
    )
    highest, totals, summed = attend_all(queries)(
        start_state,
        (
            lax.all_gather(keys, "ctx", axis=0, tiled=True),
            lax.all_gather(values, "ctx", axis=0, tiled=True),
        ),
        jnp.int32(0),
    )
    attended = (
        (summed / totals[..., None])
        .transpose(1, 0, 2)
        .reshape(local_tokens, local_heads * HDIM)
        .astype(jnp.bfloat16)
    )
    feature_count = tokens.shape[2]
    columns = w_out
    projected = (
        lax.psum_scatter(
            lax.dot_general(
                columns, attended, (((0,), (1,)), ((), ())), preferred_element_type=jnp.float32
            ).astype(jnp.bfloat16),
            "head",
            scatter_dimension=0,
            tiled=True,
        )
        .astype(jnp.float32)
        .T
    )
    gate = lax.dynamic_slice_in_dim(
        mods[2], lax.axis_index("head") * feature_count, feature_count, 0
    )
    return (gate * projected).astype(jnp.bfloat16)[None]


def solution(mesh):
    in_specs = (
        P("grp", "ctx", "head"),
        P("grp", None, None),
        P(("ctx", "grp"), None, "head"),
        P(),
        P(),
        P("head", None),
    )
    out_specs = P("grp", "ctx", "head")
    return jax.shard_map(body, mesh=mesh, in_specs=in_specs, out_specs=out_specs, check_vma=False)
```

profile of v0, /device:TPU:1, one launch (start us, length us, event | category | flops | bytes accessed | tf_op | source)
XLA Modules:
  0.0 709.8 jit_solution(13191710850817180703)
XLA Ops:
  7.3 1.5 copy.34
  10.5 37.0 %all-gather.11.cloned.1.call-done = bf16[1,256,3072]{2,1,0:T(8,128)(2,1)} async-done(((bf16[1,256,384]{2,1,0:T(8,128)(2,1)}), bf16[1,256,3072]{2,1,0:T(8,128)(2,1)}) %all-gather.11.cloned.1.call-update) | async-done | bytes 1572880 | tf_op jit(solution)/shard_map/all_gather | solution.py:57
  47.5 1.8 convert_reduce_fusion
  49.4 2.0 fusion.17
  51.3 250.8 %all-gather.7.cloned.1.call-done = bf16[3072,768]{1,0:T(8,128)(2,1)} async-done(((bf16[48,768]{1,0:T(8,128)(2,1)}), bf16[3072,768]{1,0:T(8,128)(2,1)}) %all-gather.7.cloned.1.call-update) | async-done | bytes 4718608 | tf_op jit(solution)/shard_map/all_gather | solution.py:68
  302.2 4.8 fusion.21
  307.0 1.5 reshape.61
  311.0 157.9 %all-gather.13.cloned.1.call-done = bf16[8192,1,2,128]{3,0,2,1:T(8,128)(2,1)} async-done(((bf16[256,1,2,128]{3,0,2,1:T(8,128)(2,1)}), bf16[8192,1,2,128]{3,0,2,1:T(8,128)(2,1)}) %all-gather.13.cloned.1.call-update) | async-done | bytes 4194320 | tf_op jit(solution)/shard_map/all_gather | solution.py:84
  468.9 133.4 %all-gather.9.cloned.1.call-done = bf16[8192,2,128]{2,0,1:T(8,128)(2,1)} async-done(((bf16[256,2,128]{2,0,1:T(8,128)(2,1)}), bf16[8192,2,128]{2,0,1:T(8,128)(2,1)}) %all-gather.9.cloned.1.call-update) | async-done | bytes 4194320 | tf_op jit(solution)/shard_map/all_gather | solution.py:83
  602.2 46.0 %while.15 = (s32[]{:T(128)}, f32[2,256]{1,0:T(2,128)S(1)}, f32[2,256]{1,0:T(2,128)S(1)}, f32[2,256,128]{2,1,0:T(8,128)S(1)}, bf16[16,512,2,128]{3,1,0,2:T(8,128)...) while((s32[]{:T(128)}, f32[2,256]{1,0:T(2,128)S(1)}, ...), condition=%wide.region_7.8_spmd.clone, body=%wide.region_4.7_spmd.clone.sunk | while | flops 135989760 | bytes 4358265 | solution.py:48
  603.7 1.4 convolution_add_fusion.2
  606.6 1.4 convolution_add_fusion.2
  612.3 1.4 convolution_add_fusion.2
  615.2 1.4 convolution_add_fusion.2
  618.1 1.4 convolution_add_fusion.2
  623.8 1.4 convolution_add_fusion.2
  626.7 1.4 convolution_add_fusion.2
  629.6 1.4 convolution_add_fusion.2
  635.3 1.4 convolution_add_fusion.2
  638.2 1.4 convolution_add_fusion.2
  641.1 1.4 convolution_add_fusion.2
  646.8 1.4 convolution_add_fusion.2
  649.0 1.6 copy.27
  650.7 50.8 %reduce-scatter.4.cloned.1.call-done = bf16[384,256]{1,0:T(8,128)(2,1)} async-done(((bf16[3072,256]{1,0:T(8,128)(2,1)}), bf16[384,256]{1,0:T(8,128)(2,1)}) %reduce-scatter.4.cloned.1.call-update) | async-done | bytes 196624
  (125 shorter events, 36.2 us)
Async XLA Ops:
  6.5 641.9 %copy-start = (bf16[256,3072]{1,0:T(8,128)(2,1)S(1)}, bf16[256,3072]{1,0:T(8,128)(2,1)}, u32[]{:S(2)}) copy-start(bf16[256,3072]{1,0:T(8,128)(2,1)} %param.13) | copy-start | bytes 4718596
  6.5 41.0 %all-gather.11.cloned.1.call-start = ((), (), s32[]{:S(2)}) async-start(), calls=%async_computation.3 | async-start | bytes 1769472 | tf_op jit(solution)/shard_map/all_gather | solution.py:57
  7.3 294.9 %all-gather.7.cloned.1.call-start = ((), (), s32[]{:S(2)}) async-start(), calls=%async_computation.1 | async-start | bytes 4792320 | tf_op jit(solution)/shard_map/all_gather | solution.py:68
  8.9 460.0 %all-gather.13.cloned.1.call-start = ((), (), s32[]{:S(2)}) async-start(), calls=%async_computation.4 | async-start | bytes 4325376 | tf_op jit(solution)/shard_map/all_gather | solution.py:84
  47.5 254.6 %copy-start.1 = (bf16[1,256,3072]{2,1,0:T(8,128)(2,1)S(1)}, bf16[1,256,3072]{2,1,0:T(8,128)(2,1)}, u32[]{:S(2)}) copy-start(bf16[1,256,3072]{2,1,0:T(8,128)(2,1)} %all-gather.11.cloned.1.call-done) | copy-start | bytes 4718596
  307.0 2.8 copy-start.2
  307.0 3.8 copy-start.3
  309.4 292.9 %all-gather.9.cloned.1.call-start = ((), (), s32[]{:S(2)}) async-start(), calls=%async_computation.2 | async-start | bytes 4325376 | tf_op jit(solution)/shard_map/all_gather | solution.py:83
  310.6 390.8 %reduce-scatter.4.cloned.1.call-start = ((), (), s32[]{:S(2)}) async-start(), calls=%async_computation.5 | async-start | bytes 1769472
Sparse Core Ops, SparseCore 0:
  9.5 38.0 all-gather.10
  49.6 252.4 all-gather.6
  309.5 159.3 all-gather.12
  470.8 131.3 all-gather.8
  650.8 50.6 reduce-scatter.3
where the time goes:
time: 712 us; the launch traced here: 710 us
  waiting for transfers between devices  631 us (89%)
  matrix products  47.7 us (7%)
  between operations  13.3 us (2%)
  other arithmetic  9.52 us (1%)
  local copies, waits for them, and re-layouts  7.74 us (1%)
    all_gather x1, waiting for transfers between devices, body(): lax.all_gather(weight_rows, ('ctx', 'grp'), axis=0, tiled=True)  251 us
    all_gather x1, waiting for transfers between devices, body(): lax.all_gather(values, 'ctx', axis=0, tiled=True)  158 us
    all_gather x1, waiting for transfers between devices, body(): lax.all_gather(keys, 'ctx', axis=0, tiled=True)  133 us
    unnamed x6, waiting for transfers between devices  51.6 us
    all_gather x1, waiting for transfers between devices, body(): whole = lax.all_gather(tokens[0], 'head', axis=1, tiled=True)  37 us
    dot_general x16, matrix products, block_update(): jnp.einsum('hqk,khd->hqd', weights.astype(jnp.bfloat16), block_values, pr...  22 us
    dot_general x16, matrix products, block_update(): jnp.einsum('qhd,khd->hqk', queries, block_keys, preferred_element_type=jn...  20.3 us
  transfers between devices with their start and end apart: 5, of which 5 were waited for; matrix products, arithmetic and copies ran while one was open for 1% of the time, Pallas kernels for 0%

commit v1 on v0

v1 whole, which is shorter than its diff:
```python
import functools

import jax
import jax.numpy as jnp
import numpy as np
from jax import lax
from jax.experimental import pallas as pl
from jax.experimental.pallas import tpu as pltpu
from jax.sharding import PartitionSpec as P

MESH = pl.DeviceIdType.MESH
BF16 = jnp.bfloat16
F32 = jnp.float32
NZ, NH, HDIM = 16, 8, 128
TOK, FEAT, WIDTH = 256, 384, 3072
PART = 32
QKV = 3 * HDIM
BATCHES, SLOTS = 4, 4
ROWS = SLOTS * PART
N_SEMS = 160
EXP2_SCALE = float(HDIM ** (-0.5) * np.log2(np.e))


def head_of(z):
    return lax.rem(z, 4) * 4 + z // 4


def holder_shift(z):
    return 1 - jnp.minimum(lax.rem(z, 15), 1)


def kernel(
    tok,
    mod,
    w_in,
    q_gain,
    k_gain,
    w_out,
    out,
    wp,
    ta,
    xb,
    wb,
    qb,
    kv,
    wo,
    os,
    ob,
    m_s,
    l_s,
    a_s,
    send_sem,
    recv_sem,
):
    c = lax.axis_index("ctx")
    h = lax.axis_index("head")
    yhi = lax.axis_index("grp")
    ylo, z = c // NZ, lax.rem(c, NZ)
    y = 2 * yhi + ylo

    def dev(y, z, h):
        return (lax.rem(y, 2) * NZ + z, h, y // 2)

    def at_z(k):
        return dev(y, lax.rem(z + k + NZ, NZ), h)

    def at_y(k):
        return dev(lax.rem(y + k + 4, 4), z, h)

    def head_at(k):
        return lax.rem(h + 2 * k + NH, NH)

    partner_y = dev(y + 1 - 2 * ylo, z, h)
    sibling = h + 1 - 2 * lax.rem(h, 2)
    right, left = dev(y, z, head_at(1)), dev(y, z, head_at(-1))
    core = dev(y, z, sibling)
    bits = (lax.rem(h, 2), lax.rem(h // 2, 2), h // 4)
    peers = []
    for i in range(1, NH):
        flips = (i & 1, (i >> 1) & 1, i >> 2)
        peers.append(
            sum((b + f - 2 * b * f) * w for b, f, w in zip(bits, flips, (1, 2, 4)))
        )

    count = [0]
    started = []

    def new(n=1):
        first = count[0]
        count[0] += n
        assert count[0] <= N_SEMS
        return first

    def copy(src, dst, device, recv=None, start=True):
        i = new()
        op = pltpu.make_async_remote_copy(
            src_ref=src,
            dst_ref=dst,
            send_sem=send_sem.at[i],
            recv_sem=recv_sem.at[i if recv is None else recv],
            device_id=device,
            device_id_type=MESH,
        )
        if start:
            op.start()
            started.append(op)
        return op

    my_head = head_of(z)
    piece = 4 * h + lax.rem(y + 4 - holder_shift(z), 4)
    own_piece = ylo * NZ + z
    w_targets = []
    for p in range(2):
        plane = head_of(2 * h + p)
        w_targets.append(
            dev(
                lax.rem(lax.rem(own_piece, 4) + holder_shift(plane), 4),
                plane,
                own_piece // 4,
            )
        )
    barrier = pltpu.get_barrier_semaphore()
    greet = [dev(y, z, j) for j in peers]
    greet += [at_z(k) for k in range(1, NZ)]
    greet += [at_y(1), at_y(-1)]
    greet += [(piece, my_head // 2, s) for s in range(2)]
    for d in greet:
        pl.semaphore_signal(barrier, inc=1, device_id=d, device_id_type=MESH)
    pl.semaphore_wait(barrier, len(greet))

    def rows(ref, start, size, unit):
        return ref.at[pl.ds(pl.multiple_of(start, unit), size)]

    tok_in = [
        copy(rows(tok, PART * j, PART, PART), ta.at[h], dev(y, z, j)) for j in peers
    ]
    ta[h] = tok[pl.ds(pl.multiple_of(PART * h, PART), PART), :]

    for p in range(2):
        for j in range(3):
            wp[p, :, j * HDIM : (j + 1) * HDIM] = w_in[
                :, j * 2 * HDIM + p * HDIM : j * 2 * HDIM + (p + 1) * HDIM
            ]
    w_recv = new(2)
    for p in range(2):
        copy(
            wp.at[p],
            rows(wb, 96 * own_piece + 48 * yhi, 48, 48),
            w_targets[p],
            recv=w_recv + yhi,
        )
    w_in_ops = [
        copy(
            wp.at[s],
            rows(wb, 96 * piece + 48 * s, 48, 48),
            core,
            recv=w_recv + s,
            start=False,
        )
        for s in range(2)
    ]

    wo_in = [
        copy(
            w_out.at[
                pl.ds(pl.multiple_of(64 * y, 64), 64),
                pl.ds(pl.multiple_of(FEAT * j, FEAT), FEAT),
            ],
            wo.at[h, y],
            dev(y, z, j),
        )
        for j in peers
    ]

    for op in tok_in:
        op.wait_recv()
    total = jnp.zeros((PART, 1), F32)
    for j in range(NH):
        total += jnp.sum(ta[j].astype(F32), axis=-1, keepdims=True)
    center = total / WIDTH
    total = jnp.zeros((PART, 1), F32)
    for j in range(NH):
        total += jnp.sum((ta[j].astype(F32) - center) ** 2, axis=-1, keepdims=True)
    scale = lax.rsqrt(total / WIDTH + 1e-06)
    for j in range(NH):
        cols = slice(FEAT * j, FEAT * (j + 1))
        normed = (ta[j].astype(F32) - center) * scale
        xb[0, :, cols] = (
            normed * (1.0 + mod[1:2, cols].astype(F32)) + mod[0:1, cols].astype(F32)
        ).astype(BF16)

    half = PART // 2

    def part(slot, i):
        return xb.at[slot, pl.ds(half * i, half)]

    from_left, from_right = {}, {}

    def ring_send(k):
        def one(i, rightward):
            if rightward:
                src = 0 if k == 1 else 2 * (k - 1) - 1
                dst = 2 * k - 1
            else:
                src = 0 if k == 1 else 2 * (k - 1)
                dst = 2 * k if k < 8 else 15
            op = copy(part(src, i), part(dst, i), at_z(1) if rightward else at_z(-1))
            (from_left if rightward else from_right)[k, i] = op

        if k < 8:
            for i in range(2):
                for rightward in (True, False):
                    if k > 1:
                        (from_left if rightward else from_right)[k - 1, i].wait_recv()
                    one(i, rightward)
        else:
            for i in range(2):
                from_left[7, i].wait_recv()
                if i == 0:
                    one(0, True)
                from_right[7, i].wait_recv()
                if i == 1:
                    one(1, False)

    ring_send(1)

    def project(b):
        x = xb[SLOTS * b : SLOTS * (b + 1)].reshape(ROWS, WIDTH)
        qkv = jnp.dot(x, wb[...], preferred_element_type=F32)

        def norm(v, gain):
            mean_square = jnp.mean(v * v, axis=-1, keepdims=True)
            return (v * lax.rsqrt(mean_square + 1e-06) * gain[...]).astype(BF16)

        qb[ROWS * b : ROWS * (b + 1), :] = norm(qkv[:, :HDIM], q_gain)
        mine = pl.ds(pl.multiple_of(ROWS * (2 * h + ylo), ROWS), ROWS)
        kv[b, mine, 0:HDIM] = norm(qkv[:, HDIM : 2 * HDIM], k_gain)
        kv[b, mine, HDIM : 2 * HDIM] = qkv[:, 2 * HDIM :].astype(BF16)

    def kv_rows(b, j, first=0, n=2):
        start = ROWS * (2 * j + first)
        return kv.at[b, pl.ds(pl.multiple_of(start, ROWS), ROWS * n)]

    kv_y, kv_l, kv_r, kv_fl, kv_fr, kv_c = {}, {}, {}, {}, {}, {}

    def kv_pair(b):
        kv_y[b] = copy(kv_rows(b, h, ylo, 1), kv_rows(b, h, ylo, 1), partner_y)

    def kv_own(b):
        kv_y[b].wait_recv()
        block = kv_rows(b, h)
        kv_l[b] = copy(block, block, right)
        kv_r[b] = copy(block, block, left)
        kv_c[b] = [copy(block, block, core)]

    def kv_forward(b):
        lh, rh = head_at(-1), head_at(1)
        kv_l[b].wait_recv()
        kv_fl[b] = copy(kv_rows(b, lh, 0, 1), kv_rows(b, lh, 0, 1), right)
        kv_c[b].append(copy(kv_rows(b, lh), kv_rows(b, lh), core))
        kv_r[b].wait_recv()
        kv_fr[b] = copy(kv_rows(b, rh, 1, 1), kv_rows(b, rh, 1, 1), left)
        kv_c[b].append(copy(kv_rows(b, rh), kv_rows(b, rh), core))

    def kv_last(b):
        kv_fl[b].wait_recv()
        kv_fr[b].wait_recv()
        far = kv_rows(b, head_at(2))
        kv_c[b].append(copy(far, far, core))

    def kv_done(b):
        for op in kv_c[b]:
            op.wait_recv()

    for op in w_in_ops:
        op.wait_recv()

    def w_rows(t, first=0, n=96):
        return rows(wb, 96 * t + first, n, 48)

    def w_piece(k):
        return 4 * h + lax.rem(piece + k + 4, 4)

    w_up = copy(w_rows(piece), w_rows(piece), at_y(1))
    w_down = copy(w_rows(piece), w_rows(piece), at_y(-1))

    ring_send(2)

    w_up.wait_recv()
    w_up2 = copy(w_rows(w_piece(-1), 0, 48), w_rows(w_piece(-1), 0, 48), at_y(1))
    w_down.wait_recv()
    w_down2 = copy(w_rows(w_piece(1), 48, 48), w_rows(w_piece(1), 48, 48), at_y(-1))

    ring_send(3)

    def w_block(j, first=0, n=384):
        return rows(wb, 384 * j + first, n, 192)

    w_up2.wait_recv()
    w_down2.wait_recv()
    w_l = copy(w_block(h), w_block(h), right)
    w_r = copy(w_block(h), w_block(h), left)
    w_c = [copy(w_block(h), w_block(h), core)]

    for op in wo_in:
        op.wait_recv()
    wo[h, y] = w_out[
        pl.ds(pl.multiple_of(64 * y, 64), 64),
        pl.ds(pl.multiple_of(FEAT * h, FEAT), FEAT),
    ]
    wo_up = copy(wo.at[:, y], wo.at[:, y], at_y(1))
    wo_down = copy(wo.at[:, y], wo.at[:, y], at_y(-1))

    ring_send(4)

    lh, rh = head_at(-1), head_at(1)
    w_l.wait_recv()
    w_fl = copy(w_block(lh, 0, 192), w_block(lh, 0, 192), right)
    w_c.append(copy(w_block(lh), w_block(lh), core))
    w_r.wait_recv()
    w_fr = copy(w_block(rh, 192, 192), w_block(rh, 192, 192), left)
    w_c.append(copy(w_block(rh), w_block(rh), core))

    ring_send(5)

    w_fl.wait_recv()
    w_fr.wait_recv()
    w_c.append(copy(w_block(head_at(2)), w_block(head_at(2)), core))
    for op in w_c:
        op.wait_recv()

    project(0)
    kv_pair(0)

    ring_send(6)

    project(1)
    kv_pair(1)
    kv_own(0)

    ring_send(7)

    project(2)
    kv_pair(2)
    kv_own(1)

    ring_send(8)

    kv_forward(0)
    y_up, y_down = lax.rem(y + 1, 4), lax.rem(y + 3, 4)
    wo_up.wait_recv()
    wo_up2 = copy(
        wo.at[pl.ds(0, 4), y_down], wo.at[pl.ds(0, 4), y_down], at_y(1)
    )
    wo_down.wait_recv()
    wo_down2 = copy(wo.at[pl.ds(4, 4), y_up], wo.at[pl.ds(4, 4), y_up], at_y(-1))
    kv_own(2)

    from_left[8, 0].wait_recv()
    from_right[8, 1].wait_recv()
    project(3)
    kv_pair(3)
    kv_forward(1)
    kv_last(0)
    kv_own(3)
    kv_forward(2)
    kv_last(1)
    kv_done(0)

    def attend(b):
        s = lax.dot_general(
            qb[...], kv[b, :, 0:HDIM], (((1,), (1,)), ((), ())), preferred_element_type=F32
        )
        top = jnp.max(s, axis=1, keepdims=True) * EXP2_SCALE
        if b > 0:
            before = m_s[...]
            now = jnp.maximum(before, top)
            factor = jnp.exp2(before - now)
        else:
            now = jnp.broadcast_to(top, (BATCHES * ROWS, HDIM))
        p = jnp.exp2(s * EXP2_SCALE - now[:, 0:1])
        o = jnp.dot(p.astype(BF16), kv[b, :, HDIM:], preferred_element_type=F32)
        t = jnp.sum(p, axis=1, keepdims=True)
        if b > 0:
            l_s[...] = l_s[...] * factor + t
            a_s[...] = a_s[...] * factor + o
        else:
            l_s[...] = jnp.broadcast_to(t, (BATCHES * ROWS, HDIM))
            a_s[...] = o
        m_s[...] = now

    attend(0)
    kv_forward(3)
    kv_last(2)
    kv_done(1)
    attend(1)
    kv_last(3)
    kv_done(2)
    attend(2)
    kv_done(3)
    attend(3)

    os[...] = (a_s[...] / l_s[...]).astype(BF16).reshape(NZ, PART, HDIM)

    mine = pl.ds(pl.multiple_of(HDIM * my_head, HDIM), HDIM)
    back = []
    for k in range(1, 8):
        back.append(copy(os.at[2 * k - 1], ob.at[h, :, mine], at_z(-k)))
        back.append(copy(os.at[2 * k], ob.at[h, :, mine], at_z(k)))
    back.append(copy(os.at[15], ob.at[h, :, mine], at_z(8)))
    ob[h, :, mine] = os[0]
    wo_up2.wait_recv()
    wo_down2.wait_recv()
    for op in back:
        op.wait_recv()

    def o_block(j, first=0, n=PART):
        return ob.at[j, pl.ds(first, n)]

    o_l = copy(o_block(h), o_block(h), right)
    o_r = copy(o_block(h), o_block(h), left)
    o_c = [copy(o_block(h), o_block(h), core)]
    o_l.wait_recv()
    o_fl = copy(o_block(lh, 0, 16), o_block(lh, 0, 16), right)
    o_c.append(copy(o_block(lh), o_block(lh), core))
    o_r.wait_recv()
    o_fr = copy(o_block(rh, 16, 16), o_block(rh, 16, 16), left)
    o_c.append(copy(o_block(rh), o_block(rh), core))
    o_fl.wait_recv()
    o_fr.wait_recv()
    far = head_at(2)
    o_c.append(copy(o_block(far), o_block(far), core))
    for op in o_c:
        op.wait_recv()

    projected = jnp.dot(
        ob[...].reshape(TOK, 2048),
        wo[...].reshape(2048, FEAT),
        preferred_element_type=F32,
    )
    gate = mod[2:3, pl.ds(pl.multiple_of(FEAT * h, FEAT), FEAT)].astype(F32)
    out[...] = (gate * projected).astype(BF16)

    for op in started:
        op.wait_send()


def body(tokens, modulation, w_qkv, query_gain, key_gain, w_out):
    vmem = pl.BlockSpec(memory_space=pltpu.VMEM)
    branch = pl.pallas_call(
        kernel,
        out_shape=jax.ShapeDtypeStruct((TOK, FEAT), BF16),
        in_specs=[vmem] * 6,
        out_specs=vmem,
        scratch_shapes=[
            pltpu.VMEM((2, 48, QKV), BF16),
            pltpu.VMEM((NH, PART, FEAT), BF16),
            pltpu.VMEM((NZ, PART, WIDTH), BF16),
            pltpu.VMEM((WIDTH, QKV), BF16),
            pltpu.VMEM((BATCHES * ROWS, HDIM), BF16),
            pltpu.VMEM((BATCHES, 16 * ROWS, 2 * HDIM), BF16),
            pltpu.VMEM((NH, 4, 64, FEAT), BF16),
            pltpu.VMEM((NZ, PART, HDIM), BF16),
            pltpu.VMEM((NH, PART, 2048), BF16),
            pltpu.VMEM((BATCHES * ROWS, HDIM), F32),
            pltpu.VMEM((BATCHES * ROWS, HDIM), F32),
            pltpu.VMEM((BATCHES * ROWS, HDIM), F32),
            pltpu.SemaphoreType.DMA((N_SEMS,)),
            pltpu.SemaphoreType.DMA((N_SEMS,)),
        ],
        compiler_params=pltpu.CompilerParams(
            collective_id=0, has_side_effects=True, vmem_limit_bytes=48 << 20
        ),
        name="branch",
    )(
        tokens[0],
        modulation[0],
        w_qkv.reshape(48, 6 * HDIM),
        query_gain.reshape(1, HDIM),
        key_gain.reshape(1, HDIM),
        w_out,
    )
    return branch[None]


def solution(mesh):
    in_specs = (
        P("grp", "ctx", "head"),
        P("grp", None, None),
        P(("ctx", "grp"), None, "head"),
        P(),
        P(),
        P("head", None),
    )
    out_specs = P("grp", "ctx", "head")
    return jax.shard_map(body, mesh=mesh, in_specs=in_specs, out_specs=out_specs, check_vma=False)
```

time: 712 us -> 113 us (0.16)
  waiting for transfers between devices: 631 us -> 0 us
  Pallas kernels: 0 us -> 106 us
  matrix products: 47.7 us -> 0 us
  between operations: 13.3 us -> 0.01 us
  other arithmetic: 9.52 us -> 0 us
    all_gather x4 -> x0, waiting for transfers between devices: 579 us -> none  [the longest x1 251 us: body(): lax.all_gather(weight_rows, ('ctx', 'grp'), axis=0, tiled=True)]
    pallas_call x0 -> x1, Pallas kernels: none -> 106 us  [body(): pl.pallas_call(kernel, out_shape=jax.ShapeDtypeStruct((TOK, FEAT), BF16),...]
    unnamed x6 -> x0, waiting for transfers between devices: 51.6 us -> none
    dot_general x34 -> x0, matrix products: 47.7 us -> none  [the longest x16 22 us: block_update(): jnp.einsum('hqk,khd->hqd', weights.astype(jnp.bfloat16), block_values, pr...]
  transfers between devices with their start and end apart: 5 -> 0, of which waited for: 5 -> 0; matrix products, arithmetic and copies ran while one was open for 1% -> 0% of each run, Pallas kernels for 0% -> 0%
where the time goes in v1:
time: 113 us; the launch traced here: 112 us
  Pallas kernels  106 us (94%)
  local copies, waits for them, and re-layouts  5.95 us (5%)
    pallas_call x1, Pallas kernels, body(): pl.pallas_call(kernel, out_shape=jax.ShapeDtypeStruct((TOK, FEAT), BF16),...  106 us
    unnamed x11, local copies, waits for them, and re-layouts  5.06 us

profile of v1, /device:TPU:1, one launch (start us, length us, event | category | flops | bytes accessed | tf_op | source)
XLA Modules:
  0.0 112.3 jit_solution(10548812057981492240)
XLA Ops:
  0.0 0.9 copy.9
  0.9 0.0 copy-start
  0.9 1.4 %copy-done = bf16[256,3072]{1,0:T(8,128)(2,1)S(1)} copy-done((bf16[256,3072]{1,0:T(8,128)(2,1)S(1)}, bf16[256,3072]{1,0:T(8,128)(2,1)}, u32[]{:S(2)}) %copy-start) | copy-done | bytes 1572888
  2.3 0.0 copy-start.1
  2.3 0.9 copy-done.1
  3.2 0.0 copy-start.2
  3.2 0.7 copy-done.2
  4.0 0.0 copy-start.3
  4.0 0.7 copy-done.3
  4.6 0.0 copy-start.4
  4.6 0.7 copy-done.4
  5.3 106.3 %branch.1 = bf16[256,384]{1,0:T(8,128)(2,1)S(1)} custom-call(bf16[256,384]{1,0:T(8,128)(2,1)S(1)} %bitcast.9, bf16[3,3072]{1,0:T(4,128)(2,1)S(1)} %bitcast.10, bf16[48,768]{1,0:T(8,128)(2,1)S(1)} %bitcast.8, f32[1,128]{1,0:T(1,128)S(1)} %bitcast.11, f32[1,128]{1,0:T(1,128)S(1)} %bitcast.12, bf16[256,3072]{1,0:T(8,128)(2,1)S(1)} %copy-done), custom_call_target="tpu_custom_call" | custom-call | tf_op jit(solution)/shard_map/branch/pallas_call | solution.py:450
  111.6 0.7 copy.11
Async XLA Ops:
  0.9 1.4 %copy-start = (bf16[256,3072]{1,0:T(8,128)(2,1)S(1)}, bf16[256,3072]{1,0:T(8,128)(2,1)}, u32[]{:S(2)}) copy-start(bf16[256,3072]{1,0:T(8,128)(2,1)} %w_out.1) | copy-start | bytes 4718596
  2.3 0.9 copy-start.1
  3.2 0.7 copy-start.2
  4.0 0.7 copy-start.3
  4.6 0.7 copy-start.4

commit v2 on v0

v2 whole, which is shorter than its diff:
```python
import functools

import jax
import jax.numpy as jnp
import numpy as np
from jax import lax
from jax.experimental import pallas as pl
from jax.experimental.pallas import tpu as pltpu
from jax.sharding import PartitionSpec as P

MESH = pl.DeviceIdType.MESH
BF16 = jnp.bfloat16
F32 = jnp.float32
NZ, NH, HDIM = 16, 8, 128
TOK, FEAT, WIDTH = 256, 384, 3072
PART = 32
SPLIT = (4, 4, 4, 3, 1)
FIRST = tuple(sum(SPLIT[:b]) for b in range(len(SPLIT)))
LAST = len(SPLIT) - 1
ROWS = NZ * PART
HALF = PART // 2
EARLY = ((0, 1), (1, 1))
LATE = ((2, 1), (3, 2))
N_SEMS = 240
WAYS = (1, 3, 2)
(
    W_SENT, W_HERE, TOKENS, W_OUT, BLOCK, W_A_Y, W_B_X, W_A_X, W_B_Y, W_CORE,
    KV_BLOCK, KV_CORE, W_OUT_Y, ATTENDED, HEADS, HEADS_CORE,
) = range(16)
(
    W1, SPREAD, WO, LN, RING, WD, WFA, WFB, WC, PROJ, KVF, KVC, WOY, EA, LA, BACK, O, OC, OUT,
) = range(19)
EXP2_SCALE = float(HDIM ** (-0.5) * np.log2(np.e))
ORDER = (
    (W1,), (SPREAD,), (LN,), (WO,), (RING, 2, 1, 0), (RING, 2, 0, 0), (WD,), (RING, 2, 1, 1),
    (RING, 2, 0, 1), (RING, 2, 0, 2), (RING, 2, 1, 2), (RING, 2, 0, 3), (RING, 2, 1, 3),
    (RING, 3, 0, 0), (WFA, 1), (RING, 3, 1, 0), (WFB, 3), (WFB, 1), (RING, 3, 0, 1),
    (RING, 3, 1, 1), (WFA, 3), (WFB, 2), (RING, 3, 0, 2), (RING, 3, 1, 2), (RING, 3, 0, 3),
    (WFA, 2), (RING, 3, 1, 3), (RING, 4, 0, 0), (RING, 4, 1, 0), (RING, 4, 1, 1),
    (RING, 4, 0, 1), (WC, 0), (RING, 4, 0, 2), (RING, 4, 1, 2), (WC, 3), (RING, 4, 0, 3),
    (WC, 1), (RING, 4, 1, 3), (RING, 5, 1, 0), (RING, 5, 0, 0), (WC, 2), (RING, 5, 0, 1),
    (RING, 5, 1, 1), (RING, 5, 0, 2), (RING, 5, 1, 2), (PROJ, 0), (RING, 5, 0, 3),
    (RING, 5, 1, 3), (PROJ, 1), (RING, 6, 0, 0), (RING, 6, 1, 0), (RING, 6, 0, 1),
    (RING, 6, 1, 1), (RING, 6, 0, 2), (RING, 6, 1, 2), (RING, 6, 0, 3), (RING, 6, 1, 3),
    (KVF, 0), (RING, 7, 0, 0), (RING, 7, 1, 0), (RING, 7, 1, 1), (RING, 7, 0, 1),
    (RING, 7, 1, 2), (KVF, 1), (RING, 7, 0, 2), (RING, 7, 1, 3), (RING, 7, 0, 3), (PROJ, 2),
    (RING, 8, 0, 0), (KVC, 0, 1), (KVC, 0, 3), (RING, 8, 0, 1), (RING, 8, 1, 2), (KVC, 0, 2),
    (KVC, 1, 3), (RING, 8, 1, 3), (KVF, 2), (PROJ, 3), (KVC, 1, 2), (EA, 0, 0), (KVC, 1, 1),
    (PROJ, 4), (EA, 1, 0), (KVF, 3), (KVC, 2, 1), (KVC, 2, 3), (EA, 1, 1), (KVC, 2, 2),
    (EA, 0, 1), (WOY,), (KVC, 4, 0), (KVC, 4, 1), (KVC, 4, 3), (KVC, 4, 2), (KVC, 3, 1),
    (KVC, 3, 3), (LA, 0, 0), (KVC, 3, 2), (LA, 1, 0), (LA, 0, 1), (BACK, 0), (LA, 1, 1),
    (BACK, 1), (O, 0), (O, 1), (OC, 0, 1), (OC, 0, 3), (OC, 0, 2), (OC, 1, 1), (OC, 1, 3),
    (OC, 1, 2), (OUT,),
)


def head_of(z):
    return lax.rem(z, 4) * 4 + z // 4


def kernel(
    tok,
    mod_hbm,
    w_in,
    q_gain_hbm,
    k_gain_hbm,
    w_out,
    out,
    mod,
    q_gain,
    k_gain,
    wp,
    ta,
    xb,
    wb,
    qb,
    kv,
    wo,
    os,
    ob,
    m_s,
    l_s,
    a_s,
    local_sem,
    send_sem,
    recv_sem,
):
    c = lax.axis_index("ctx")
    h = lax.axis_index("head")
    yhi = lax.axis_index("grp")
    ylo, z = c // NZ, lax.rem(c, NZ)
    y = 2 * yhi + ylo

    def dev(y, z, h):
        return (lax.rem(y, 2) * NZ + z, h, y // 2)

    def at_z(k):
        return dev(y, lax.rem(z + k + NZ, NZ), h)

    def at_y(k):
        return dev(lax.rem(y + k + 4, 4), z, h)

    def head_at(k):
        return lax.rem(h + 2 * k + NH, NH)

    def at(dx, dy):
        return dev(lax.rem(y + dy, 4), z, head_at(dx))

    other_y = y + 1 - 2 * ylo
    core = dev(y, z, h + 1 - 2 * lax.rem(h, 2))
    bits = (lax.rem(h, 2), lax.rem(h // 2, 2), h // 4)
    peers = []
    for i in range(NH):
        flips = (i & 1, (i >> 1) & 1, i >> 2)
        peers.append(
            sum((b + f - 2 * b * f) * w for b, f, w in zip(bits, flips, (1, 2, 4)))
        )

    count = [0]
    started = []
    ops = {}

    def copy(name, src, dst, device, recv=None, start=True):
        i = count[0]
        count[0] += 1
        assert i < N_SEMS
        op = pltpu.make_async_remote_copy(
            src_ref=src,
            dst_ref=dst,
            send_sem=send_sem.at[i],
            recv_sem=recv_sem.at[i if recv is None else recv],
            device_id=device,
            device_id_type=MESH,
        )
        if start:
            op.start()
            started.append(op)
        assert name not in ops
        ops[name] = op

    waited = set()

    def wait(*names):
        for name in names:
            if name not in waited:
                waited.add(name)
                ops[name].wait_recv()

    def rows(ref, start, size, unit):
        return ref.at[pl.ds(pl.multiple_of(start, unit), size)]

    def span(start, size):
        return pl.ds(pl.multiple_of(start, size), size)

    my_head = head_of(z)
    piece = lax.rem(h + 4, NH)
    w_targets = [
        dev(y, head_of(2 * h + p), lax.rem(z // 2 + 4, NH)) for p in range(2)
    ]

    locals_ = []

    def local(src, dst):
        op = pltpu.make_async_copy(src, dst, local_sem.at[len(locals_)])
        op.start()
        locals_.append(op)
        return op

    wp_ops = [
        local(
            w_in.at[j, :, pl.ds(p * HDIM, HDIM)],
            wp.at[p, :, pl.ds(j * HDIM, HDIM)],
        )
        for p in range(2)
        for j in range(3)
    ]
    tok_own = local(rows(tok, PART * h, PART, PART), ta.at[h])
    mod_op = local(mod_hbm, mod)
    gain_ops = [local(q_gain_hbm, q_gain), local(k_gain_hbm, k_gain)]
    wo_own = local(w_out.at[span(64 * y, 64), span(FEAT * h, FEAT)], wo.at[h, y])

    barrier = pltpu.get_barrier_semaphore()
    greet = [dev(y, z, peers[i]) for i in range(1, NH)]
    greet += [at_z(k) for k in range(1, NZ)]
    greet += [at(dx, dy) for dx in range(4) for dy in WAYS]
    greet += [dev(y, 2 * piece + s, my_head // 2) for s in range(2)]
    for d in greet:
        pl.semaphore_signal(barrier, inc=1, device_id=d, device_id_type=MESH)
    pl.semaphore_wait(barrier, len(greet))

    tasks = {}

    def task(*name):
        def add(f):
            tasks[name] = f
            return f

        return add

    @task(W1)
    def _():
        for op in wp_ops:
            op.wait()
        base = count[0]
        for p in range(2):
            copy(
                (W_SENT, p),
                wp.at[p],
                wb.at[ylo, z // 2, lax.rem(z, 2), yhi],
                w_targets[p],
                recv=base + lax.rem(z, 2),
            )
        for s in range(2):
            copy(
                (W_HERE, s),
                wp.at[s],
                wb.at[ylo, piece, s, yhi],
                core,
                recv=base + s,
                start=False,
            )

    def w_half(dx, dy, s):
        yy = lax.rem(y + dy, 4)
        return wb.at[lax.rem(yy, 2), lax.rem(head_at(dx) + 4, NH), s, yy // 2]

    def w_send(name, block, dx, dy):
        copy(name, block, block, at(dx, dy))

    @task(WD)
    def _():
        wait((W_HERE, 0), (W_HERE, 1))
        for d in WAYS:
            w_send((W_A_Y, 4 - d), w_half(0, 0, 0), 0, d)
        for d in WAYS:
            w_send((W_B_X, 4 - d), w_half(0, 0, 1), d, 0)
        for d in WAYS:
            w_send((W_A_X, 4 - d, 0), w_half(0, 0, 0), d, 0)
        for d in WAYS:
            w_send((W_B_Y, 0, 4 - d), w_half(0, 0, 1), 0, d)

    def add_w_forward(d):
        @task(WFA, d)
        def _():
            wait((W_A_Y, d))
            for dx in WAYS:
                w_send((W_A_X, 4 - dx, d), w_half(0, d, 0), dx, 0)

        @task(WFB, d)
        def _():
            wait((W_B_X, d))
            for dy in WAYS:
                w_send((W_B_Y, d, 4 - dy), w_half(d, 0, 1), 0, dy)

    for d in WAYS:
        add_w_forward(d)

    def w_names(dx):
        if dx == 0:
            names = [(W_A_Y, dy) for dy in WAYS]
        else:
            names = [(W_B_X, dx)] + [(W_A_X, dx, dy) for dy in range(4)]
        return names + [(W_B_Y, dx, dy) for dy in WAYS]

    def add_w_core(dx):
        @task(WC, dx)
        def _():
            wait(*w_names(dx))
            block = wb.at[:, lax.rem(head_at(dx) + 4, NH)]
            copy((W_CORE, dx), block, block, core)

    for dx in range(4):
        add_w_core(dx)

    @task(SPREAD)
    def _():
        for i in range(1, NH):
            copy(
                (TOKENS, i),
                rows(tok, PART * peers[i], PART, PART),
                ta.at[h],
                dev(y, z, peers[i]),
            )

    @task(WO)
    def _():
        for i in range(1, NH):
            copy(
                (W_OUT, i),
                w_out.at[span(64 * y, 64), span(FEAT * peers[i], FEAT)],
                wo.at[h, y],
                dev(y, z, peers[i]),
            )

    @task(LN)
    def _():
        wait(*((TOKENS, i) for i in range(1, NH)))
        tok_own.wait()
        mod_op.wait()
        total = jnp.zeros((PART, 1), F32)
        for j in range(NH):
            total += jnp.sum(ta[j].astype(F32), axis=-1, keepdims=True)
        center = total / WIDTH
        total = jnp.zeros((PART, 1), F32)
        for j in range(NH):
            total += jnp.sum((ta[j].astype(F32) - center) ** 2, axis=-1, keepdims=True)
        scale = lax.rsqrt(total / WIDTH + 1e-06)
        for j in range(NH):
            cols = slice(FEAT * j, FEAT * (j + 1))
            normed = (ta[j].astype(F32) - center) * scale
            xb[0, :, cols] = (
                normed * (1.0 + mod[1:2, cols].astype(F32)) + mod[0:1, cols].astype(F32)
            ).astype(BF16)
        for i in range(4):
            ring_copy(1, 0, i)
            ring_copy(1, 1, i)

    def ring_copy(k, way, i):
        step = min(2 * k - 1 + way, 15)
        before = 0 if k == 1 else 2 * k - 3 + way
        half = pl.ds(PART // 2 * (i // 2), PART // 2)
        cols = pl.ds(WIDTH // 2 * (i % 2), WIDTH // 2)
        copy(
            (BLOCK, way, k, i),
            xb.at[before, half, cols],
            xb.at[step, half, cols],
            at_z(1 - 2 * way),
        )

    def add_ring(k, way, i):
        @task(RING, k, way, i)
        def _():
            wait((BLOCK, way, k - 1, i))
            ring_copy(k, way, i)

    for k in range(2, 9):
        for way in range(2):
            for i in range(4):
                if k < 8 or (way == 0) == (i < 2):
                    add_ring(k, way, i)

    def slot_names(s):
        if s == 0:
            return []
        if s == 15:
            return [(BLOCK, 0, 8, 0), (BLOCK, 0, 8, 1), (BLOCK, 1, 8, 2), (BLOCK, 1, 8, 3)]
        way, k = 1 - s % 2, (s + 1) // 2
        return [(BLOCK, way, k, i) for i in range(4)]

    @task(WOY)
    def _():
        wait(*((W_OUT, i) for i in range(1, NH)))
        wo_own.wait()
        for dy in WAYS:
            copy((W_OUT_Y, dy), wo.at[:, y], wo.at[:, y], at(0, dy))

    def kv_slot(b, j, yl):
        n = PART * SPLIT[b]
        return pl.ds(pl.multiple_of(NZ * PART * FIRST[b] + n * (2 * j + yl), PART), n)

    def add_batch(b):
        first, n = PART * FIRST[b], PART * SPLIT[b]

        def norm(v, gain):
            mean_square = jnp.mean(v * v, axis=-1, keepdims=True)
            return (v * lax.rsqrt(mean_square + 1e-06) * gain[...]).astype(BF16)

        @task(PROJ, b)
        def _():
            for dx in range(4):
                wait(*w_names(dx), (W_CORE, dx))
            for s in range(FIRST[b], FIRST[b] + SPLIT[b]):
                wait(*slot_names(s))
            if b == 0:
                for op in gain_ops:
                    op.wait()
            x = xb[FIRST[b] : FIRST[b] + SPLIT[b]].reshape(n, WIDTH)
            w = wb[...].reshape(WIDTH, 3 * HDIM)
            qkv = jnp.dot(x, w, preferred_element_type=F32)
            here = kv_slot(b, h, ylo)
            kv[here, 0:HDIM] = norm(qkv[:, HDIM : 2 * HDIM], k_gain)
            kv[here, HDIM : 2 * HDIM] = qkv[:, 2 * HDIM :].astype(BF16)
            mine = kv.at[here]
            qs = norm(qkv[:, :HDIM], q_gain).reshape(SPLIT[b], 2, HALF, HDIM)
            for yy in range(2 if b == LAST else 1):
                for dx in (0,) + WAYS:
                    if dx or yy:
                        there = dev(other_y if yy else y, z, head_at(dx))
                        copy((KV_BLOCK, b, (4 - dx) % 4, yy), mine, mine, there)
            if b < LAST:
                copy((KV_BLOCK, b, 0, 1), mine, mine, dev(other_y, z, h))
            for i in range(2):
                qb[i, HALF * FIRST[b] : HALF * (FIRST[b] + SPLIT[b])] = qs[:, i].reshape(
                    n // 2, HDIM
                )

        def pair(dx):
            start = NZ * first + 2 * n * head_at(dx)
            return rows(kv, start, 2 * n, PART)

        if b < LAST:

            @task(KVF, b)
            def _():
                wait((KV_BLOCK, b, 0, 1))
                block = kv.at[kv_slot(b, h, 1 - ylo)]
                for dx in WAYS:
                    copy((KV_BLOCK, b, 4 - dx, 1), block, block, at(dx, 0))
                copy((KV_CORE, b, 0), pair(0), pair(0), core)

        def add_core(dx):
            @task(KVC, b, dx)
            def _():
                wait(*((KV_BLOCK, b, dx, yy) for yy in range(2) if dx or yy))
                copy((KV_CORE, b, dx), pair(dx), pair(dx), core)

        for dx in WAYS if b < LAST else range(4):
            add_core(dx)

    for b in range(LAST + 1):
        add_batch(b)

    def kv_names(b):
        names = [(KV_BLOCK, b, dx, yy) for dx in range(4) for yy in range(2) if dx or yy]
        return names + [(KV_CORE, b, dx) for dx in range(4)]

    def attend(batches, where, start, end):
        b, n = batches
        for i in range(n):
            wait(*kv_names(b + i))
        keys = pl.ds(NZ * PART * FIRST[b], NZ * PART * sum(SPLIT[b : b + n]))

        def get(ref):
            return ref[where].reshape(ROWS // 2, HDIM)

        def put(ref, value):
            ref[where] = value.reshape(ref[where].shape)

        s = lax.dot_general(
            get(qb),
            kv[keys, 0:HDIM],
            (((1,), (1,)), ((), ())),
            preferred_element_type=F32,
        )
        top = jnp.max(s, axis=1, keepdims=True) * EXP2_SCALE
        if start:
            now = jnp.broadcast_to(top, (ROWS // 2, HDIM))
        else:
            before = get(m_s)
            now = jnp.maximum(before, top)
            factor = jnp.exp2(before - now)
        p = jnp.exp2(s * EXP2_SCALE - now[:, 0:1])
        o = jnp.dot(p.astype(BF16), kv[keys, HDIM:], preferred_element_type=F32)
        t = jnp.broadcast_to(jnp.sum(p, axis=1, keepdims=True), (ROWS // 2, HDIM))
        if not start:
            t += get(l_s) * factor
            o += get(a_s) * factor
        if end:
            put(os, (o / t).astype(BF16))
        else:
            put(m_s, now)
            put(l_s, t)
            put(a_s, o)

    def add_attention(g, j, early):
        @task(EA if early else LA, g, j)
        def _():
            if early:
                slots = slice(ROWS // 4 * g, ROWS // 4 * (g + 1))
                attend(EARLY[j], (slice(None), slots), j == 0, False)
            else:
                attend(LATE[j], g, not EARLY and j == 0, j == len(LATE) - 1)

    for g in range(2):
        for j in range(len(EARLY)):
            add_attention(g, j, True)
        for j in range(len(LATE)):
            add_attention(g, j, False)

    head_cols = span(HDIM * my_head, HDIM)

    def add_return(g):
        half = pl.ds(HALF * g, HALF)

        @task(BACK, g)
        def _():
            for s in reversed(range(NZ)):
                here = os.at[g, pl.ds(HALF * s, HALF)]
                if s == 0:
                    ob[h, half, head_cols] = os[g, 0:HALF]
                    continue
                k = 8 if s == 15 else (-((s + 1) // 2) if s % 2 else s // 2)
                copy((ATTENDED, g, s), here, ob.at[h, half, head_cols], at_z(k))

        @task(O, g)
        def _():
            wait(*((ATTENDED, g, s) for s in range(1, NZ)))
            block = ob.at[h, half]
            copy((HEADS_CORE, g, 0), block, block, core)
            for dx in WAYS:
                copy((HEADS, g, 4 - dx), block, block, at(dx, 0))

        def add_core(dx):
            @task(OC, g, dx)
            def _():
                wait((HEADS, g, dx))
                block = ob.at[head_at(dx), half]
                copy((HEADS_CORE, g, dx), block, block, core)

        for dx in WAYS:
            add_core(dx)

    for g in range(2):
        add_return(g)

    @task(OUT)
    def _():
        wait(*((W_OUT_Y, dy) for dy in WAYS))
        wait(*((HEADS_CORE, g, dx) for g in range(2) for dx in range(4)))
        projected = jnp.dot(
            ob[...].reshape(TOK, 2048),
            wo[...].reshape(2048, FEAT),
            preferred_element_type=F32,
        )
        gate = mod[2:3, span(FEAT * h, FEAT)].astype(F32)
        out[...] = (gate * projected).astype(BF16)

    assert set(ORDER) == set(tasks) and len(ORDER) == len(tasks)
    for name in ORDER:
        tasks[name]()
    for op in started:
        op.wait_send()


def body(tokens, modulation, w_qkv, query_gain, key_gain, w_out):
    branch = pl.pallas_call(
        kernel,
        out_shape=jax.ShapeDtypeStruct((TOK, FEAT), BF16),
        in_specs=[pl.BlockSpec(memory_space=pltpu.HBM)] * 6,
        out_specs=pl.BlockSpec(memory_space=pltpu.VMEM),
        scratch_shapes=[
            pltpu.VMEM((3, WIDTH), BF16),
            pltpu.VMEM((1, HDIM), F32),
            pltpu.VMEM((1, HDIM), F32),
            pltpu.VMEM((2, 48, 3 * HDIM), BF16),
            pltpu.VMEM((NH, PART, FEAT), BF16),
            pltpu.VMEM((NZ, PART, WIDTH), BF16),
            pltpu.VMEM((2, NH, 2, 2, 48, 3 * HDIM), BF16),
            pltpu.VMEM((2, ROWS // 2, HDIM), BF16),
            pltpu.VMEM((NZ * ROWS, 2 * HDIM), BF16),
            pltpu.VMEM((NH, 4, 64, FEAT), BF16),
            pltpu.VMEM((2, ROWS // 2, HDIM), BF16),
            pltpu.VMEM((NH, PART, 2048), BF16),
            pltpu.VMEM((2, ROWS // 2, HDIM), F32),
            pltpu.VMEM((2, ROWS // 2, HDIM), F32),
            pltpu.VMEM((2, ROWS // 2, HDIM), F32),
            pltpu.SemaphoreType.DMA((16,)),
            pltpu.SemaphoreType.DMA((N_SEMS,)),
            pltpu.SemaphoreType.DMA((N_SEMS,)),
        ],
        compiler_params=pltpu.CompilerParams(
            collective_id=0, has_side_effects=True, vmem_limit_bytes=60 << 20
        ),
        name="branch",
    )(
        tokens[0],
        modulation[0],
        w_qkv.transpose(1, 0, 2),
        query_gain.reshape(1, HDIM),
        key_gain.reshape(1, HDIM),
        w_out,
    )
    return branch[None]


def solution(mesh):
    in_specs = (
        P("grp", "ctx", "head"),
        P("grp", None, None),
        P(("ctx", "grp"), None, "head"),
        P(),
        P(),
        P("head", None),
    )
    out_specs = P("grp", "ctx", "head")
    return jax.shard_map(body, mesh=mesh, in_specs=in_specs, out_specs=out_specs, check_vma=False)
```

time: 712 us -> 96.7 us (0.14)
  waiting for transfers between devices: 631 us -> 0 us
  Pallas kernels: 0 us -> 94.9 us
  matrix products: 47.7 us -> 0 us
  between operations: 13.3 us -> 0.01 us
  other arithmetic: 9.52 us -> 0 us
    all_gather x4 -> x0, waiting for transfers between devices: 579 us -> none  [the longest x1 251 us: body(): lax.all_gather(weight_rows, ('ctx', 'grp'), axis=0, tiled=True)]
    pallas_call x0 -> x1, Pallas kernels: none -> 94.9 us  [body(): pl.pallas_call(kernel, out_shape=jax.ShapeDtypeStruct((TOK, FEAT), BF16),...]
    unnamed x6 -> x0, waiting for transfers between devices: 51.6 us -> none
    dot_general x34 -> x0, matrix products: 47.7 us -> none  [the longest x16 22 us: block_update(): jnp.einsum('hqk,khd->hqd', weights.astype(jnp.bfloat16), block_values, pr...]
  transfers between devices with their start and end apart: 5 -> 0, of which waited for: 5 -> 0; matrix products, arithmetic and copies ran while one was open for 1% -> 0% of each run, Pallas kernels for 0% -> 0%
where the time goes in v2:
time: 96.7 us; the launch traced here: 96.6 us
  Pallas kernels  94.9 us (98%)
  local copies, waits for them, and re-layouts  1.62 us (2%)
    pallas_call x1, Pallas kernels, body(): pl.pallas_call(kernel, out_shape=jax.ShapeDtypeStruct((TOK, FEAT), BF16),...  94.9 us

profile of v2, /device:TPU:1, one launch (start us, length us, event | category | flops | bytes accessed | tf_op | source)
XLA Modules:
  0.0 96.6 jit_solution(18173310964589591880)
XLA Ops:
  0.0 94.9 %branch.1 = bf16[256,384]{1,0:T(8,128)(2,1)} custom-call(bf16[256,384]{1,0:T(8,128)(2,1)} %bitcast.7, bf16[3,3072]{1,0:T(4,128)(2,1)} %bitcast.9, bf16[3,48,256]{2,1,0:T(8,128)(2,1)} %bitcast.8, f32[1,128]{1,0:T(1,128)} %bitcast.10, f32[1,128]{1,0:T(1,128)} %bitcast.11, bf16[256,3072]{1,0:T(8,128)(2,1)} %w_out.1), custom_call_target="tpu_custom_call" | custom-call | tf_op jit(solution)/shard_map/branch/pallas_call | solution.py:536
  94.9 1.6 %copy.8 = bf16[1,256,384]{2,1,0:T(8,128)(2,1)} copy(bf16[1,256,384]{2,1,0:T(8,128)(2,1)} %bitcast.6) | data formatting | bytes 393216

commit v3 on v2

--- a/solution.py
+++ b/solution.py
@@ -17,10 +17,12 @@
 SPLIT = (4, 4, 4, 3, 1)
 FIRST = tuple(sum(SPLIT[:b]) for b in range(len(SPLIT)))
 LAST = len(SPLIT) - 1
+Y_FIRST, X_FIRST, STRAIGHT = range(3)
+WAY_OF = (X_FIRST, Y_FIRST, STRAIGHT, STRAIGHT, STRAIGHT)
 ROWS = NZ * PART
 HALF = PART // 2
-EARLY = ((0, 1), (1, 1))
-LATE = ((2, 1), (3, 2))
+EARLY = ((0, 1), (1, 1), (2, 1))
+LATE = ((3, 2),)
 N_SEMS = 240
 WAYS = (1, 3, 2)
 (
@@ -32,25 +34,25 @@
 ) = range(19)
 EXP2_SCALE = float(HDIM ** (-0.5) * np.log2(np.e))
 ORDER = (
-    (W1,), (SPREAD,), (LN,), (WO,), (RING, 2, 1, 0), (RING, 2, 0, 0), (WD,), (RING, 2, 1, 1),
-    (RING, 2, 0, 1), (RING, 2, 0, 2), (RING, 2, 1, 2), (RING, 2, 0, 3), (RING, 2, 1, 3),
-    (RING, 3, 0, 0), (WFA, 1), (RING, 3, 1, 0), (WFB, 3), (WFB, 1), (RING, 3, 0, 1),
-    (RING, 3, 1, 1), (WFA, 3), (WFB, 2), (RING, 3, 0, 2), (RING, 3, 1, 2), (RING, 3, 0, 3),
-    (WFA, 2), (RING, 3, 1, 3), (RING, 4, 0, 0), (RING, 4, 1, 0), (RING, 4, 1, 1),
-    (RING, 4, 0, 1), (WC, 0), (RING, 4, 0, 2), (RING, 4, 1, 2), (WC, 3), (RING, 4, 0, 3),
-    (WC, 1), (RING, 4, 1, 3), (RING, 5, 1, 0), (RING, 5, 0, 0), (WC, 2), (RING, 5, 0, 1),
-    (RING, 5, 1, 1), (RING, 5, 0, 2), (RING, 5, 1, 2), (PROJ, 0), (RING, 5, 0, 3),
+    (W1,), (SPREAD,), (WO,), (LN,), (RING, 2, 0, 0), (RING, 2, 1, 0), (WD,), (RING, 2, 0, 1),
+    (RING, 2, 1, 1), (RING, 2, 0, 2), (RING, 2, 1, 2), (RING, 2, 0, 3), (RING, 2, 1, 3),
+    (WFA, 1), (WFB, 1), (WFA, 3), (WFB, 3), (RING, 3, 0, 0), (RING, 3, 1, 0), (RING, 3, 0, 1),
+    (RING, 3, 1, 1), (WFA, 2), (WFB, 2), (RING, 3, 0, 2), (RING, 3, 1, 2), (WC, 0),
+    (RING, 3, 0, 3), (RING, 3, 1, 3), (RING, 4, 0, 0), (RING, 4, 1, 0), (RING, 4, 0, 1),
+    (RING, 4, 1, 1), (RING, 4, 0, 2), (RING, 4, 1, 2), (WC, 1), (WC, 3), (RING, 4, 0, 3),
+    (RING, 4, 1, 3), (WC, 2), (RING, 5, 0, 0), (RING, 5, 1, 0), (RING, 5, 0, 1),
+    (RING, 5, 1, 1), (PROJ, 0), (RING, 5, 0, 2), (RING, 5, 1, 2), (RING, 5, 0, 3),
     (RING, 5, 1, 3), (PROJ, 1), (RING, 6, 0, 0), (RING, 6, 1, 0), (RING, 6, 0, 1),
-    (RING, 6, 1, 1), (RING, 6, 0, 2), (RING, 6, 1, 2), (RING, 6, 0, 3), (RING, 6, 1, 3),
-    (KVF, 0), (RING, 7, 0, 0), (RING, 7, 1, 0), (RING, 7, 1, 1), (RING, 7, 0, 1),
-    (RING, 7, 1, 2), (KVF, 1), (RING, 7, 0, 2), (RING, 7, 1, 3), (RING, 7, 0, 3), (PROJ, 2),
-    (RING, 8, 0, 0), (KVC, 0, 1), (KVC, 0, 3), (RING, 8, 0, 1), (RING, 8, 1, 2), (KVC, 0, 2),
-    (KVC, 1, 3), (RING, 8, 1, 3), (KVF, 2), (PROJ, 3), (KVC, 1, 2), (EA, 0, 0), (KVC, 1, 1),
-    (PROJ, 4), (EA, 1, 0), (KVF, 3), (KVC, 2, 1), (KVC, 2, 3), (EA, 1, 1), (KVC, 2, 2),
-    (EA, 0, 1), (WOY,), (KVC, 4, 0), (KVC, 4, 1), (KVC, 4, 3), (KVC, 4, 2), (KVC, 3, 1),
-    (KVC, 3, 3), (LA, 0, 0), (KVC, 3, 2), (LA, 1, 0), (LA, 0, 1), (BACK, 0), (LA, 1, 1),
-    (BACK, 1), (O, 0), (O, 1), (OC, 0, 1), (OC, 0, 3), (OC, 0, 2), (OC, 1, 1), (OC, 1, 3),
-    (OC, 1, 2), (OUT,),
+    (RING, 6, 1, 1), (KVF, 0, 1), (KVF, 0, 3), (KVC, 0, 0), (RING, 6, 0, 2), (RING, 6, 1, 2),
+    (RING, 6, 0, 3), (KVF, 1, 0), (RING, 6, 1, 3), (RING, 7, 0, 0), (RING, 7, 1, 0),
+    (KVF, 0, 2), (KVC, 0, 1), (RING, 7, 0, 1), (RING, 7, 1, 1), (RING, 7, 0, 2),
+    (RING, 7, 1, 2), (PROJ, 2), (KVC, 0, 3), (RING, 8, 0, 0), (KVC, 1, 3), (RING, 7, 1, 3),
+    (KVC, 0, 2), (KVC, 1, 1), (RING, 7, 0, 3), (KVC, 1, 2), (RING, 8, 0, 1), (RING, 8, 1, 2),
+    (EA, 0, 0), (RING, 8, 1, 3), (PROJ, 3), (KVC, 2, 0), (EA, 0, 1), (KVC, 2, 1), (PROJ, 4),
+    (KVC, 2, 3), (KVC, 2, 2), (KVC, 3, 0), (WOY,), (EA, 1, 0), (EA, 0, 2), (KVC, 4, 0),
+    (KVC, 3, 1), (KVC, 3, 3), (EA, 1, 1), (KVC, 3, 2), (KVC, 4, 1), (KVC, 4, 3), (KVC, 4, 2),
+    (EA, 1, 2), (LA, 0, 0), (BACK, 0), (LA, 1, 0), (BACK, 1), (O, 0), (O, 1), (OC, 0, 1),
+    (OC, 0, 3), (OC, 0, 2), (OC, 1, 1), (OC, 1, 3), (OUT, 0), (OC, 1, 2), (OUT, 1),
 )
 
 
@@ -134,9 +136,15 @@
         )
         if start:
             op.start()
-            started.append(op)
+            started.append((name, op))
         assert name not in ops
         ops[name] = op
+
+    def drain(*later):
+        for name, op in started:
+            if name[0] not in later:
+                op.wait_send()
+        started[:] = [sent for sent in started if sent[0][0] in later]
 
     waited = set()
 
@@ -382,12 +390,12 @@
             kv[here, HDIM : 2 * HDIM] = qkv[:, 2 * HDIM :].astype(BF16)
             mine = kv.at[here]
             qs = norm(qkv[:, :HDIM], q_gain).reshape(SPLIT[b], 2, HALF, HDIM)
-            for yy in range(2 if b == LAST else 1):
+            for yy in range(2 if WAY_OF[b] == STRAIGHT else 1):
                 for dx in (0,) + WAYS:
                     if dx or yy:
                         there = dev(other_y if yy else y, z, head_at(dx))
                         copy((KV_BLOCK, b, (4 - dx) % 4, yy), mine, mine, there)
-            if b < LAST:
+            if WAY_OF[b] != STRAIGHT:
                 copy((KV_BLOCK, b, 0, 1), mine, mine, dev(other_y, z, h))
             for i in range(2):
                 qb[i, HALF * FIRST[b] : HALF * (FIRST[b] + SPLIT[b])] = qs[:, i].reshape(
@@ -398,9 +406,9 @@
             start = NZ * first + 2 * n * head_at(dx)
             return rows(kv, start, 2 * n, PART)
 
-        if b < LAST:
-
-            @task(KVF, b)
+        if WAY_OF[b] == Y_FIRST:
+
+            @task(KVF, b, 0)
             def _():
                 wait((KV_BLOCK, b, 0, 1))
                 block = kv.at[kv_slot(b, h, 1 - ylo)]
@@ -408,13 +416,24 @@
                     copy((KV_BLOCK, b, 4 - dx, 1), block, block, at(dx, 0))
                 copy((KV_CORE, b, 0), pair(0), pair(0), core)
 
+        def add_forward(dx):
+            @task(KVF, b, dx)
+            def _():
+                wait((KV_BLOCK, b, dx, 0))
+                block = kv.at[kv_slot(b, head_at(dx), ylo)]
+                copy((KV_BLOCK, b, dx, 1), block, block, dev(other_y, z, h))
+
+        if WAY_OF[b] == X_FIRST:
+            for dx in WAYS:
+                add_forward(dx)
+
         def add_core(dx):
             @task(KVC, b, dx)
             def _():
                 wait(*((KV_BLOCK, b, dx, yy) for yy in range(2) if dx or yy))
                 copy((KV_CORE, b, dx), pair(dx), pair(dx), core)
 
-        for dx in WAYS if b < LAST else range(4):
+        for dx in WAYS if WAY_OF[b] == Y_FIRST else range(4):
             add_core(dx)
 
     for b in range(LAST + 1):
@@ -494,6 +513,7 @@
 
         @task(O, g)
         def _():
+            drain(W_OUT_Y, ATTENDED, HEADS, HEADS_CORE)
             wait(*((ATTENDED, g, s) for s in range(1, NZ)))
             block = ob.at[h, half]
             copy((HEADS_CORE, g, 0), block, block, core)
@@ -513,29 +533,35 @@
     for g in range(2):
         add_return(g)
 
-    @task(OUT)
-    def _():
-        wait(*((W_OUT_Y, dy) for dy in WAYS))
-        wait(*((HEADS_CORE, g, dx) for g in range(2) for dx in range(4)))
-        projected = jnp.dot(
-            ob[...].reshape(TOK, 2048),
-            wo[...].reshape(2048, FEAT),
-            preferred_element_type=F32,
-        )
-        gate = mod[2:3, span(FEAT * h, FEAT)].astype(F32)
-        out[...] = (gate * projected).astype(BF16)
+    def add_out(g):
+        @task(OUT, g)
+        def _():
+            wait(*((W_OUT_Y, dy) for dy in WAYS))
+            wait(*((HEADS_CORE, g, dx) for dx in range(4)))
+            half = slice(HALF * g, HALF * (g + 1))
+            projected = jnp.dot(
+                ob[:, half].reshape(TOK // 2, 2048),
+                wo[...].reshape(2048, FEAT),
+                preferred_element_type=F32,
+            )
+            gate = mod[2:3, span(FEAT * h, FEAT)].astype(F32)
+            out[:, half] = (gate * projected).astype(BF16).reshape(NH, HALF, FEAT)
+            if g == 0:
+                drain(W_OUT_Y, HEADS, HEADS_CORE)
+
+    for g in range(2):
+        add_out(g)
 
     assert set(ORDER) == set(tasks) and len(ORDER) == len(tasks)
     for name in ORDER:
         tasks[name]()
-    for op in started:
-        op.wait_send()
+    drain()
 
 
 def body(tokens, modulation, w_qkv, query_gain, key_gain, w_out):
     branch = pl.pallas_call(
         kernel,
-        out_shape=jax.ShapeDtypeStruct((TOK, FEAT), BF16),
+        out_shape=jax.ShapeDtypeStruct((NH, PART, FEAT), BF16),
         in_specs=[pl.BlockSpec(memory_space=pltpu.HBM)] * 6,
         out_specs=pl.BlockSpec(memory_space=pltpu.VMEM),
         scratch_shapes=[
@@ -570,7 +596,7 @@
         key_gain.reshape(1, HDIM),
         w_out,
     )
-    return branch[None]
+    return branch.reshape(1, TOK, FEAT)
 
 
 def solution(mesh):

time: 96.7 us -> 96.3 us (level)
  no operation moved by 1% of the time
where the time goes in v3:
time: 96.3 us; the launch traced here: 96.2 us
  Pallas kernels  94.6 us (98%)
  local copies, waits for them, and re-layouts  1.62 us (2%)
    pallas_call x1, Pallas kernels, body(): pl.pallas_call(kernel, out_shape=jax.ShapeDtypeStruct((NH, PART, FEAT), B...  94.6 us

profile of v3, /device:TPU:1, one launch (start us, length us, event | category | flops | bytes accessed | tf_op | source)
XLA Modules:
  0.0 96.2 jit_solution(8234331086751522615)
XLA Ops:
  0.0 94.6 %branch.1 = bf16[8,32,384]{2,1,0:T(8,128)(2,1)} custom-call(bf16[256,384]{1,0:T(8,128)(2,1)} %bitcast.7, bf16[3,3072]{1,0:T(4,128)(2,1)} %bitcast.9, bf16[3,48,256]{2,1,0:T(8,128)(2,1)} %bitcast.8, f32[1,128]{1,0:T(1,128)} %bitcast.10, f32[1,128]{1,0:T(1,128)} %bitcast.11, bf16[256,3072]{1,0:T(8,128)(2,1)} %w_out.1), custom_call_target="tpu_custom_call" | custom-call | tf_op jit(solution)/shard_map/branch/pallas_call | solution.py:562
  94.6 1.6 %copy.8 = bf16[1,256,384]{2,1,0:T(8,128)(2,1)} copy(bf16[1,256,384]{2,1,0:T(8,128)(2,1)} %bitcast.6) | data formatting | bytes 393216

commit v4 on v3

--- a/solution.py
+++ b/solution.py
@@ -49,7 +49,7 @@
     (RING, 7, 1, 2), (PROJ, 2), (KVC, 0, 3), (RING, 8, 0, 0), (KVC, 1, 3), (RING, 7, 1, 3),
     (KVC, 0, 2), (KVC, 1, 1), (RING, 7, 0, 3), (KVC, 1, 2), (RING, 8, 0, 1), (RING, 8, 1, 2),
     (EA, 0, 0), (RING, 8, 1, 3), (PROJ, 3), (KVC, 2, 0), (EA, 0, 1), (KVC, 2, 1), (PROJ, 4),
-    (KVC, 2, 3), (KVC, 2, 2), (KVC, 3, 0), (WOY,), (EA, 1, 0), (EA, 0, 2), (KVC, 4, 0),
+    (KVC, 2, 3), (KVC, 2, 2), (KVC, 3, 0), (EA, 1, 0), (WOY,), (EA, 0, 2), (KVC, 4, 0),
     (KVC, 3, 1), (KVC, 3, 3), (EA, 1, 1), (KVC, 3, 2), (KVC, 4, 1), (KVC, 4, 3), (KVC, 4, 2),
     (EA, 1, 2), (LA, 0, 0), (BACK, 0), (LA, 1, 0), (BACK, 1), (O, 0), (O, 1), (OC, 0, 1),
     (OC, 0, 3), (OC, 0, 2), (OC, 1, 1), (OC, 1, 3), (OUT, 0), (OC, 1, 2), (OUT, 1),

time: 96.3 us -> 95.7 us (level)
  no operation moved by 1% of the time
where the time goes in v4:
time: 95.7 us; the launch traced here: 95.6 us
  Pallas kernels  93.9 us (98%)
  local copies, waits for them, and re-layouts  1.62 us (2%)
    pallas_call x1, Pallas kernels, body(): pl.pallas_call(kernel, out_shape=jax.ShapeDtypeStruct((NH, PART, FEAT), B...  93.9 us

profile of v4, /device:TPU:1, one launch (start us, length us, event | category | flops | bytes accessed | tf_op | source)
XLA Modules:
  0.0 95.6 jit_solution(9720294389257371421)
XLA Ops:
  0.0 93.9 %branch.1 = bf16[8,32,384]{2,1,0:T(8,128)(2,1)} custom-call(bf16[256,384]{1,0:T(8,128)(2,1)} %bitcast.7, bf16[3,3072]{1,0:T(4,128)(2,1)} %bitcast.9, bf16[3,48,256]{2,1,0:T(8,128)(2,1)} %bitcast.8, f32[1,128]{1,0:T(1,128)} %bitcast.10, f32[1,128]{1,0:T(1,128)} %bitcast.11, bf16[256,3072]{1,0:T(8,128)(2,1)} %w_out.1), custom_call_target="tpu_custom_call" | custom-call | tf_op jit(solution)/shard_map/branch/pallas_call | solution.py:562
  94.0 1.6 %copy.8 = bf16[1,256,384]{2,1,0:T(8,128)(2,1)} copy(bf16[1,256,384]{2,1,0:T(8,128)(2,1)} %bitcast.6) | data formatting | bytes 393216
